TPU v7x, 256 devices: a whole 4x4x8 slice. The times are simulated.
256 devices in a mesh: wide: 32 (over x, y, core), narrow: 8 (over z).
Axes of the slice: x: 4, y: 4, z: 8, core: 2. Of those that a mesh axis runs over, the one named last changes fastest.
Arguments:
- tokens: bfloat16 [16384, 4096], P('wide', 'narrow'), may hold values from -40 to 40
- norm_gain: float32 [4096], P('narrow'), may hold values from 0.5 to 5
- w_query: bfloat16 [4096, 4096], P(None, 'narrow'), may hold values from -0.09375 to 0.09375
- key_weight: bfloat16 [4096, 1024], P(None, 'narrow'), may hold values from -0.09375 to 0.09375
- value_weight: bfloat16 [4096, 1024], P(None, 'narrow'), may hold values from -0.09375 to 0.09375
- w_out: bfloat16 [4096, 4096], P('narrow'), may hold values from -0.09375 to 0.09375
- doc_lengths: int32 [64], replicated, may hold values from 1 to 8192, 16384 in all
Outputs:
- attended: bfloat16 [16384, 4096], P('wide', 'narrow')
Inputs may be any that keep to these rules, and one draw needn't show every extreme that they name: `doc_lengths`: the lengths sum to 16384; the longest is exactly 8192.
All inputs are finite; a program needn't handle non-finite values.
Results may differ from a plain program's by a relative error of at most 0.019.
The roundings to bfloat16 on the way count: a program that leaves them out, or rounds other values in their place, can miss the bound.
Values may be sent and summed in bfloat16 or wider, within the bound.
No kernel may reach another device: no remote copies, remote signals or barrier semaphores. Data moves between devices by JAX's collectives and lax.ppermute only.
A program may use at most 128 MiB of HBM per device.

v0:
```python
import math
import jax
import jax.numpy as jnp
from jax import lax
from jax.sharding import PartitionSpec as P

MODEL_WIDTH = 4096
HEAD_SIZE = 128
EPSILON = 1e-05
ROPE_BASE = 500000.0
NEGATIVE = -1e30


def doc_of(lengths, positions):
    starts = jnp.cumsum(lengths) - lengths
    return jnp.sum((starts[None, :] <= positions[:, None]).astype(jnp.int32), axis=1) - 1


def doc_info(lengths, positions):
    starts = jnp.cumsum(lengths) - lengths
    docs = doc_of(lengths, positions)
    onehot = docs[:, None] == jnp.arange(lengths.shape[0], dtype=jnp.int32)[None, :]
    first_tok = jnp.sum(jnp.where(onehot, starts[None, :], 0), axis=1)
    return (docs, positions - first_tok)


def apply_rotary(values, rotary_positions):
    half_width = values.shape[-1] // 2
    frequency = ROPE_BASE ** (-(jnp.arange(half_width, dtype=jnp.float32) * 2.0 / values.shape[-1]))
    angles = rotary_positions.astype(jnp.float32)[:, None] * frequency[None, :]
    cosine = jnp.cos(angles)[:, None, :]
    sine_part = jnp.sin(angles)[:, None, :]
    first_half = values[..., :half_width]
    second_half = values[..., half_width:]
    return jnp.concatenate(
        [
            first_half * cosine - second_half * sine_part,
            second_half * cosine + first_half * sine_part,
        ],
        axis=-1,
    )


def per_device(tokens, norm_gain, w_query, key_weight, value_weight, w_out, doc_lengths):
    tok_rows = tokens.shape[0]
    wide_index = lax.axis_index("wide")
    as_float = tokens.astype(jnp.float32)
    squares = lax.psum(jnp.sum(as_float * as_float, axis=1), "narrow")
    inverse = lax.rsqrt(squares / MODEL_WIDTH + EPSILON)
    normed = (as_float * inverse[:, None] * norm_gain[None, :]).astype(jnp.bfloat16)
    shard_piece = lax.all_gather(normed, "narrow", axis=1, tiled=True)
    query_raw, key_unrotated, value_projected = tuple(
        (
            jnp.dot(shard_piece, matrix, preferred_element_type=jnp.float32)
            for matrix in (w_query, key_weight, value_weight)
        )
    )
    positions = wide_index * tok_rows + jnp.arange(tok_rows, dtype=jnp.int32)
    own_doc, rotary_positions = doc_info(doc_lengths, positions)
    heads_local = w_query.shape[1] // HEAD_SIZE
    kv_local = key_weight.shape[1] // HEAD_SIZE
    heads_per_group = heads_local // kv_local
    queries_own = (
        apply_rotary(query_raw.reshape(tok_rows, heads_local, HEAD_SIZE), rotary_positions)
        .astype(jnp.bfloat16)
        .reshape(tok_rows, kv_local, heads_per_group, HEAD_SIZE)
    )
    rotated_keys = apply_rotary(
        key_unrotated.reshape(tok_rows, kv_local, HEAD_SIZE), rotary_positions
    ).astype(jnp.bfloat16)
    values_cast = value_projected.reshape(tok_rows, kv_local, HEAD_SIZE).astype(jnp.bfloat16)
    key_value = jnp.stack([rotated_keys, values_cast])
    score_scale = 1.0 / math.sqrt(HEAD_SIZE)
    last_pos = jnp.max(positions)
    first_doc = jnp.min(own_doc)

    def update(carried, key_tile, value_tile, key_pos, key_doc):
        run_max, run_sum, accum = carried
        scores = (
            jnp.einsum("rkgd,nkd->kgrn", queries_own, key_tile, preferred_element_type=jnp.float32)
            * score_scale
        )
        allowed = (key_doc[None, :] == own_doc[:, None]) & (key_pos[None, :] <= positions[:, None])
        masked = jnp.where(allowed, scores, NEGATIVE)
        new_max = jnp.maximum(run_max, jnp.max(masked, axis=-1))
        weights = jnp.where(allowed, jnp.exp(scores - new_max[..., None]), 0.0)
        factor = jnp.exp(run_max - new_max)
        run_sum = run_sum * factor + jnp.sum(weights, axis=-1)
        accum = accum * factor[..., None] + jnp.einsum(
            "kgrn,nkd->kgrd",
            weights.astype(jnp.bfloat16),
            value_tile,
            preferred_element_type=jnp.float32,
        )
        return (new_max, run_sum, accum)

    start_status = (
        jnp.full((kv_local, heads_per_group, tok_rows), NEGATIVE, jnp.float32),
        jnp.zeros((kv_local, heads_per_group, tok_rows), jnp.float32),
        jnp.zeros((kv_local, heads_per_group, tok_rows, HEAD_SIZE), jnp.float32),
    )
    pair = lax.all_gather(key_value, "wide", axis=1, tiled=True)
    count_keys = pair.shape[1]
    tile_width = math.gcd(count_keys, 512)
    tile_count = count_keys // tile_width

    def tile_step(tile_index, carried_in):
        offset = tile_index * tile_width
        key_tile = lax.dynamic_slice_in_dim(pair, offset, tile_width, 1)
        key_pos = offset + jnp.arange(tile_width, dtype=jnp.int32)
        key_doc = doc_of(doc_lengths, key_pos)
        needed = (key_pos[0] <= last_pos) & (key_doc[-1] >= first_doc)
        return lax.cond(
            needed,
            lambda status: update(status, key_tile[0], key_tile[1], key_pos, key_doc),
            lambda status: status,
            carried_in,
        )

    status_now = lax.fori_loop(0, tile_count, tile_step, start_status)
    run_max, run_sum, accum = status_now
    heads_out = (
        (accum / run_sum[..., None])
        .transpose(2, 0, 1, 3)
        .reshape(tok_rows, heads_local * HEAD_SIZE)
        .astype(jnp.bfloat16)
    )
    partial_out = jnp.dot(heads_out, w_out, preferred_element_type=jnp.float32)
    return lax.psum_scatter(
        partial_out.astype(jnp.bfloat16), "narrow", scatter_dimension=1, tiled=True
    )


def solution(mesh):
    in_specs = (
        P("wide", "narrow"),
        P("narrow"),
        P(None, "narrow"),
        P(None, "narrow"),
        P(None, "narrow"),
        P("narrow", None),
        P(),
    )
    out_specs = P("wide", "narrow")
    return jax.shard_map(
        per_device, mesh=mesh, in_specs=in_specs, out_specs=out_specs, check_vma=False
    )
```

profile of v0, /device:TPU:1, one launch (start us, length us, event | category | flops | bytes accessed | tf_op | source)
XLA Modules:
  0.0 502.4 jit_solution(14981264105822187456)
XLA Ops:
  6.5 1.3 fusion.25
  7.8 17.3 %psum.7 = f32[512]{0:T(512)S(1)} all-reduce(f32[512]{0:T(512)S(1)} %fusion.25), channel_id=1, replica_groups=mesh['wide'=32,'narrow'=8] {'narrow'}, use_global_device_ids=true, to_apply=%region_1.0 | all-reduce | flops 512 | bytes 4096 | tf_op jit(solution)/shard_map/psum | solution.py:48
  25.2 2.0 fusion.27
  27.3 0.8 copy.22
  28.3 0.7 sub.52
  29.1 0.7 broadcast_add_fusion.2
  29.9 54.0 %all-gather.3.cloned.1.call-done = bf16[512,4096]{1,0:T(8,128)(2,1)} async-done(((bf16[512,512]{1,0:T(8,128)(2,1)}), bf16[512,4096]{1,0:T(8,128)(2,1)}) %all-gather.3.cloned.1.call-update) | async-done | bytes 4194320 | tf_op jit(solution)/shard_map/all_gather | solution.py:51
  83.9 3.8 convolution_bitcast_fusion
  87.7 0.6 fusion.39
  88.3 1.5 fusion.24
  89.8 0.7 pad_maximum_fusion.1
  90.8 0.7 fusion.40
  91.5 1.7 multiply_cosine_fusion
  93.2 5.8 %fusion.43 = f32[512,512]{0,1:T(8,128)S(1)} fusion(bf16[512,4096]{1,0:T(8,128)(2,1)} %all-gather.3.cloned.1.call-done, bf16[4096,512]{1,0:T(8,128)(2,1)} %param.13), kind=kOutput, calls=%fused_computation.71 | convolution fusion | flops 2147483648 | bytes 9437184 | tf_op jit(solution)/shard_map/dot_general | solution.py:54
  99.1 0.9 fusion.42
  100.3 1.4 copy.31
  101.7 1.2 fusion.28
  103.2 51.1 %all-gather.5.cloned.1.call-done = bf16[2,16384,1,128]{1,3,2,0:T(8,128)(2,1)} async-done(((bf16[2,512,1,128]{1,3,2,0:T(8,128)(2,1)}), bf16[2,16384,1,128]{1,3,2,0:T(8,128)(2,1)}) %all-gather.5.cloned.1.call-update) | async-done | bytes 8388624 | tf_op jit(solution)/shard_map/all_gather | solution.py:102
  154.3 11.9 %copy.26 = bf16[2,16384,1,128]{3,1,2,0:T(8,128)(2,1)} copy(bf16[2,16384,1,128]{1,3,2,0:T(8,128)(2,1)} %all-gather.5.cloned.1.call-done) | data formatting | bytes 16777216
  166.3 134.6 %while.20 = (s32[]{:T(128)}, f32[1,4,512]{2,1,0:T(4,128)S(1)}, f32[1,4,512]{2,1,0:T(4,128)S(1)}, f32[1,4,512,128]{3,2,1,0:T(8,128)S(1)}, s32[]{:T(128)}, /*index...) while((s32[]{:T(128)}, f32[1,4,512]{2,1,0:T(4,128)S(1)}, ...), condition=%wide.region_13.14_spmd.clone, body=%wide.region_7.13_spmd.clone.sunk | while | flops 549821440 | bytes 33448608 | solution.py:120
  169.9 8.8 %conditional.3 = ((f32[1,4,512]{2,1,0:T(4,128)S(1)}, f32[1,4,512]{2,1,0:T(4,128)S(1)}, f32[1,4,512,128]{3,2,1,0:T(8,128)S(1)})) conditional(s32[]{:T(128)} %convert_element_type.114, (f32[1,4,512]{2,1,0:T(4,128)S(1)}, f32[1,4,512]{2,1,0:T(4,128)S(1)}, f32[1,4,512,128]{3,2,1,0:T(8,128)S(1)}) %tuple.65, (s32[512]{0:T(512)S(1)}, s32[512]{0:T(512)S(1)}, ...), branch_computations={%region_9.9_spmd, %region_10.12_spmd} | conditional | flops 549722624 | bytes 33435770 | solution.py:113
  170.2 3.7 fusion.2
  174.0 3.8 fusion.14
  177.8 0.9 fusion.6
  182.4 8.8 %conditional.3 = ((f32[1,4,512]{2,1,0:T(4,128)S(1)}, f32[1,4,512]{2,1,0:T(4,128)S(1)}, f32[1,4,512,128]{3,2,1,0:T(8,128)S(1)})) conditional(s32[]{:T(128)} %convert_element_type.114, (f32[1,4,512]{2,1,0:T(4,128)S(1)}, f32[1,4,512]{2,1,0:T(4,128)S(1)}, f32[1,4,512,128]{3,2,1,0:T(8,128)S(1)}) %tuple.65, (s32[512]{0:T(512)S(1)}, s32[512]{0:T(512)S(1)}, ...), branch_computations={%region_9.9_spmd, %region_10.12_spmd} | conditional | flops 549722624 | bytes 33435770 | solution.py:113
  182.7 3.7 fusion.2
  186.5 3.8 fusion.14
  190.3 0.9 fusion.6
  300.9 1.3 copy.27
  302.2 1.4 divide_convert_fusion
  303.6 6.5 %convolution_convert_fusion = bf16[512,4096]{1,0:T(8,128)(2,1)} fusion(bf16[512,512]{0,1:T(8,128)(2,1)S(1)} %bitcast.96, bf16[512,4096]{1,0:T(8,128)(2,1)} %param.16), kind=kOutput, calls=%fused_computation.30 | convolution fusion | flops 2149580800 | bytes 8912896 | tf_op jit(solution)/shard_map/dot_general | solution.py:128
  310.1 185.8 %reduce-scatter.2.cloned.1.call-done = bf16[512,512]{1,0:T(8,128)(2,1)} async-done(((bf16[512,4096]{1,0:T(8,128)(2,1)}), bf16[512,512]{1,0:T(8,128)(2,1)}) %reduce-scatter.2.cloned.1.call-update) | async-done | bytes 524304 | tf_op jit(solution)/shard_map/reduce_scatter | solution.py:129
  (261 shorter events, 39.1 us)
Async XLA Ops:
  6.5 77.4 %copy-start = (bf16[4096,128]{1,0:T(8,128)(2,1)S(1)}, bf16[4096,128]{1,0:T(8,128)(2,1)}, u32[]{:S(2)}) copy-start(bf16[4096,128]{1,0:T(8,128)(2,1)} %param.14) | copy-start | bytes 3145732
  6.5 77.4 %all-gather.3.cloned.1.call-start = ((), (), s32[]{:S(2)}) async-start(), calls=%async_computation.1 | async-start | bytes 4718592 | tf_op jit(solution)/shard_map/all_gather | solution.py:51
  27.2 61.1 %copy-start.3 = (bf16[4096,128]{1,0:T(8,128)(2,1)S(1)}, bf16[4096,128]{1,0:T(8,128)(2,1)}, u32[]{:S(2)}) copy-start(bf16[4096,128]{1,0:T(8,128)(2,1)} %param.15) | copy-start | bytes 3145732
  27.2 127.1 %all-gather.5.cloned.1.call-start = ((), (), s32[]{:S(2)}) async-start(), calls=%async_computation.2 | async-start | bytes 8650752 | tf_op jit(solution)/shard_map/all_gather | solution.py:102
  83.9 4.4 copy-start.2
  90.6 405.3 %reduce-scatter.2.cloned.1.call-start = ((), (), s32[]{:S(2)}) async-start(), calls=%async_computation.3 | async-start | bytes 4718592 | tf_op jit(solution)/shard_map/reduce_scatter | solution.py:129
  174.0 3.8 copy-start.1
  186.5 3.8 copy-start.1
Sparse Core Ops, SparseCore 0:
  27.3 56.5 all-gather.2
  90.7 63.5 all-gather.4
  310.2 185.6 reduce-scatter.1
where the time goes:
time: 505 us; the launch traced here: 502 us
  waiting for transfers between devices  291 us (58%)
  loops' own time  80.4 us (16%)
  local copies, waits for them, and re-layouts  50.1 us (10%)
  matrix products  32.8 us (6%)
  other arithmetic  17.4 us (3%)
  blocking collectives  17.3 us (3%)
  between operations  13.2 us (3%)
    reduce_scatter x1, waiting for transfers between devices, per_device(): lax.psum_scatter(partial_out.astype(jnp.bfloat16), 'narrow', scatter_dime...  186 us
    another operation x1, loops' own time, per_device(): status_now = lax.fori_loop(0, tile_count, tile_step, start_status)  79.9 us
    all_gather x1, waiting for transfers between devices, per_device(): shard_piece = lax.all_gather(normed, 'narrow', axis=1, tiled=True)  54 us
    all_gather x1, waiting for transfers between devices, per_device(): pair = lax.all_gather(key_value, 'wide', axis=1, tiled=True)  51.1 us
    slice x64, local copies, waits for them, and re-layouts, tile_step(): needed = (key_pos[0] <= last_pos) & (key_doc[-1] >= first_doc)  33.3 us
    psum x1, blocking collectives, per_device(): squares = lax.psum(jnp.sum(as_float * as_float, axis=1), 'narrow')  17.3 us
    unnamed x9, local copies, waits for them, and re-layouts  13.6 us
    dot_general x3, matrix products, per_device(): jnp.dot(shard_piece, matrix, preferred_element_type=jnp.float32)  11.2 us
  transfers between devices with their start and end apart: 3, of which 3 were waited for; matrix products, arithmetic and copies ran while one was open for 3% of the time, Pallas kernels for 0%

commit v1 on v0

--- a/solution.py
+++ b/solution.py
@@ -3,6 +3,7 @@
 import jax.numpy as jnp
 from jax import lax
 from jax.sharding import PartitionSpec as P
+from jax.lax import all_to_all, axis_size
 
 MODEL_WIDTH = 4096
 HEAD_SIZE = 128
@@ -48,7 +49,10 @@
     squares = lax.psum(jnp.sum(as_float * as_float, axis=1), "narrow")
     inverse = lax.rsqrt(squares / MODEL_WIDTH + EPSILON)
     normed = (as_float * inverse[:, None] * norm_gain[None, :]).astype(jnp.bfloat16)
-    shard_piece = lax.all_gather(normed, "narrow", axis=1, tiled=True)
+    shard_piece = jnp.concatenate(
+        all_to_all(jnp.stack([normed for _ in range(axis_size("narrow"))], axis=0), "narrow", 0, 0),
+        axis=1,
+    )
     query_raw, key_unrotated, value_projected = tuple(
         (
             jnp.dot(shard_piece, matrix, preferred_element_type=jnp.float32)

time: 505 us -> 544 us (1.077)
  waiting for transfers between devices: 291 us -> 314 us
  local copies, waits for them, and re-layouts: 50.1 us -> 71.5 us
    all_to_all x0 -> x1, waiting for transfers between devices: none -> 89.5 us  [per_device(): all_to_all(jnp.stack([normed for _ in range(axis_size('narrow'))], axis=0...]
    all_gather x1 -> x0, waiting for transfers between devices: 54 us -> none  [per_device(): shard_piece = lax.all_gather(normed, 'narrow', axis=1, tiled=True)]
    reshape x0 -> x3, local copies, waits for them, and re-layouts: none -> 16.7 us  [per_device(): jnp.concatenate(all_to_all(jnp.stack([normed for _ in range(axis_size('na...]
    all_gather x1, waiting for transfers between devices: 51.1 us -> 39.1 us  [per_device(): pair = lax.all_gather(key_value, 'wide', axis=1, tiled=True)]
    dot_general x0 -> x1, local copies, waits for them, and re-layouts: none -> 6.45 us  [per_device(): jnp.dot(shard_piece, matrix, preferred_element_type=jnp.float32)]
    unnamed x9 -> x10, local copies, waits for them, and re-layouts: 13.6 us -> 12.2 us
  transfers between devices with their start and end apart: 3 -> 3, of which waited for: 3 -> 3; matrix products, arithmetic and copies ran while one was open for 3% -> 5% of each run, Pallas kernels for 0% -> 0%
where the time goes in v1:
time: 544 us; the launch traced here: 541 us
  waiting for transfers between devices  314 us (58%)
  loops' own time  76.9 us (14%)
  local copies, waits for them, and re-layouts  71.5 us (13%)
  matrix products  30.6 us (6%)
  blocking collectives  17.3 us (3%)
  between operations  13.6 us (2%)
  other arithmetic  12.1 us (2%)
    reduce_scatter x1, waiting for transfers between devices, per_device(): lax.psum_scatter(partial_out.astype(jnp.bfloat16), 'narrow', scatter_dime...  186 us
    all_to_all x1, waiting for transfers between devices, per_device(): all_to_all(jnp.stack([normed for _ in range(axis_size('narrow'))], axis=0...  89.5 us
    another operation x1, loops' own time, per_device(): status_now = lax.fori_loop(0, tile_count, tile_step, start_status)  76.3 us
    all_gather x1, waiting for transfers between devices, per_device(): pair = lax.all_gather(key_value, 'wide', axis=1, tiled=True)  39.1 us
    slice x64, local copies, waits for them, and re-layouts, tile_step(): needed = (key_pos[0] <= last_pos) & (key_doc[-1] >= first_doc)  33.3 us
    psum x1, blocking collectives, per_device(): squares = lax.psum(jnp.sum(as_float * as_float, axis=1), 'narrow')  17.3 us
    reshape x3, local copies, waits for them, and re-layouts, per_device(): jnp.concatenate(all_to_all(jnp.stack([normed for _ in range(axis_size('na...  16.7 us
    unnamed x10, local copies, waits for them, and re-layouts  12.2 us
  transfers between devices with their start and end apart: 3, of which 3 were waited for; matrix products, arithmetic and copies ran while one was open for 5% of the time, Pallas kernels for 0%

profile of v1, /device:TPU:1, one launch (start us, length us, event | category | flops | bytes accessed | tf_op | source)
XLA Modules:
  0.0 541.4 jit_solution(10826953725475290016)
XLA Ops:
  6.5 1.3 fusion.25
  7.8 17.3 %psum.7 = f32[512]{0:T(512)S(1)} all-reduce(f32[512]{0:T(512)S(1)} %fusion.25), channel_id=1, replica_groups=mesh['wide'=32,'narrow'=8] {'narrow'}, use_global_device_ids=true, to_apply=%region_1.0 | all-reduce | flops 512 | bytes 4096 | tf_op jit(solution)/shard_map/psum | solution.py:49
  25.2 1.2 fusion.27
  26.4 2.3 stack.6
  28.7 4.7 all-to-all-start
  33.9 0.6 broadcast_add_fusion.2
  34.7 89.5 %all-to-all-done = bf16[8,512,512]{2,1,0:T(8,128)(2,1)} async-done(((bf16[8,512,512]{2,1,0:T(8,128)(2,1)}), bf16[8,512,512]{2,1,0:T(8,128)(2,1)}, u32[]{:S(2)}, u32[]{:S(2)}) %all-to-all-start) | async-done | bytes 4194336 | tf_op jit(solution)/shard_map/all_to_all | solution.py:53
  124.1 2.8 copy.40
  127.0 1.5 convolution_bitcast_fusion
  128.5 1.5 fusion.24
  130.0 0.6 fusion.39
  130.6 0.7 pad_maximum_fusion.1
  131.6 0.6 fusion.40
  132.2 6.5 %copy.39 = bf16[512,4096]{1,0:T(8,128)(2,1)} copy(bf16[512,4096]{0,1:T(8,128)(2,1)} %bitcast.100) | data formatting | bytes 8388608 | tf_op jit(solution)/shard_map/dot_general | solution.py:58
  139.2 6.5 %copy.31 = bf16[512,8,512]{2,1,0:T(8,128)(2,1)} copy(bf16[512,8,512]{2,0,1:T(8,128)(2,1)} %bitcast.16) | data formatting | bytes 8388608 | tf_op jit(solution)/shard_map/reshape | solution.py:52
  145.7 7.4 %reshape.306 = bf16[512,4096,1]{1,0,2:T(8,128)(2,1)} reshape(bf16[512,8,512]{2,1,0:T(8,128)(2,1)} %copy.31) | data formatting | bytes 8388608 | tf_op jit(solution)/shard_map/reshape | solution.py:52
  153.1 5.9 %fusion.42 = f32[512,4,128]{0,2,1:T(8,128)S(1)} fusion(bf16[512,4096,1]{1,0,2:T(8,128)(2,1)} %reshape.306, bf16[4,128,4096]{2,1,0:T(8,128)(2,1)} %bitcast.101), kind=kOutput, calls=%fused_computation.70 | convolution fusion | flops 2147483648 | bytes 9437184 | tf_op jit(solution)/shard_map/dot_general | solution.py:58
  159.5 39.1 %all-gather.2.cloned.1.call-done = bf16[2,16384,1,128]{1,3,2,0:T(8,128)(2,1)} async-done(((bf16[2,512,1,128]{1,3,2,0:T(8,128)(2,1)}), bf16[2,16384,1,128]{1,3,2,0:T(8,128)(2,1)}) %all-gather.2.cloned.1.call-update) | async-done | bytes 8388624 | tf_op jit(solution)/shard_map/all_gather | solution.py:106
  198.6 11.9 %copy.34 = bf16[2,16384,1,128]{3,1,2,0:T(8,128)(2,1)} copy(bf16[2,16384,1,128]{1,3,2,0:T(8,128)(2,1)} %all-gather.2.cloned.1.call-done) | data formatting | bytes 16777216
  210.6 131.0 %while.20 = (s32[]{:T(128)}, f32[1,4,512]{2,1,0:T(4,128)S(1)}, f32[1,4,512]{2,1,0:T(4,128)S(1)}, f32[1,4,512,128]{3,2,1,0:T(8,128)S(1)}, s32[]{:T(128)}, /*index...) while((s32[]{:T(128)}, f32[1,4,512]{2,1,0:T(4,128)S(1)}, ...), condition=%wide.region_13.14_spmd.clone, body=%wide.region_7.13_spmd.clone.sunk | while | flops 549821440 | bytes 33448608 | solution.py:124
  210.7 0.6 slice.77
  214.1 8.9 %conditional.3 = ((f32[1,4,512]{2,1,0:T(4,128)S(1)}, f32[1,4,512]{2,1,0:T(4,128)S(1)}, f32[1,4,512,128]{3,2,1,0:T(8,128)S(1)})) conditional(s32[]{:T(128)} %convert_element_type.114, (f32[1,4,512]{2,1,0:T(4,128)S(1)}, f32[1,4,512]{2,1,0:T(4,128)S(1)}, f32[1,4,512,128]{3,2,1,0:T(8,128)S(1)}) %tuple.65, (s32[512]{0:T(512)S(1)}, s32[512]{0:T(512)S(1)}, ...), branch_computations={%region_9.9_spmd, %region_10.12_spmd} | conditional | flops 549722624 | bytes 33435770 | solution.py:117
  214.4 3.7 fusion.2
  218.2 3.8 fusion.14
  222.0 0.9 fusion.6
  223.1 0.6 slice.77
  226.5 8.8 %conditional.3 = ((f32[1,4,512]{2,1,0:T(4,128)S(1)}, f32[1,4,512]{2,1,0:T(4,128)S(1)}, f32[1,4,512,128]{3,2,1,0:T(8,128)S(1)})) conditional(s32[]{:T(128)} %convert_element_type.114, (f32[1,4,512]{2,1,0:T(4,128)S(1)}, f32[1,4,512]{2,1,0:T(4,128)S(1)}, f32[1,4,512,128]{3,2,1,0:T(8,128)S(1)}) %tuple.65, (s32[512]{0:T(512)S(1)}, s32[512]{0:T(512)S(1)}, ...), branch_computations={%region_9.9_spmd, %region_10.12_spmd} | conditional | flops 549722624 | bytes 33435770 | solution.py:117
  226.8 3.7 fusion.2
  230.6 3.8 fusion.14
  234.4 0.9 fusion.6
  342.1 6.6 %convolution_convert_fusion = bf16[512,4096]{1,0:T(8,128)(2,1)} fusion(bf16[512,512]{0,1:T(8,128)(2,1)S(1)} %bitcast.104, bf16[512,4096]{1,0:T(8,128)(2,1)} %param.16), kind=kOutput, calls=%fused_computation.30 | convolution fusion | flops 2149580800 | bytes 8912896 | tf_op jit(solution)/shard_map/dot_general | solution.py:132
  348.7 185.8 %reduce-scatter.2.cloned.1.call-done = bf16[512,512]{1,0:T(8,128)(2,1)} async-done(((bf16[512,4096]{1,0:T(8,128)(2,1)}), bf16[512,512]{1,0:T(8,128)(2,1)}) %reduce-scatter.2.cloned.1.call-update) | async-done | bytes 524304 | tf_op jit(solution)/shard_map/reduce_scatter | solution.py:133
  (265 shorter events, 38.9 us)
Async XLA Ops:
  6.5 120.4 %copy-start = (bf16[4096,128]{1,0:T(8,128)(2,1)S(1)}, bf16[4096,128]{1,0:T(8,128)(2,1)}, u32[]{:S(2)}) copy-start(bf16[4096,128]{1,0:T(8,128)(2,1)} %param.14) | copy-start | bytes 3145732
  28.7 4.7 copy-start.4
  28.7 95.4 %all-to-all-start = ((bf16[8,512,512]{2,1,0:T(8,128)(2,1)}), bf16[8,512,512]{2,1,0:T(8,128)(2,1)}, u32[]{:S(2)}, u32[]{:S(2)}) async-start(bf16[8,512,512]{2,1,0:T(8,128)(2,1)} %stack.6), calls=%async_computation | async-start | bytes 8388608 | tf_op jit(solution)/shard_map/all_to_all | solution.py:53
  33.4 165.2 %all-gather.2.cloned.1.call-start = ((), (), s32[]{:S(2)}) async-start(), calls=%async_computation.2 | async-start | bytes 8650752 | tf_op jit(solution)/shard_map/all_gather | solution.py:106
  126.9 1.6 copy-start.3
  131.4 403.2 %reduce-scatter.2.cloned.1.call-start = ((), (), s32[]{:S(2)}) async-start(), calls=%async_computation.3 | async-start | bytes 4718592 | tf_op jit(solution)/shard_map/reduce_scatter | solution.py:133
  218.2 3.8 copy-start.2
  230.6 3.8 copy-start.2
  342.1 192.4 %copy-start.1 = (bf16[4096,128]{1,0:T(8,128)(2,1)S(1)}, bf16[4096,128]{1,0:T(8,128)(2,1)}, u32[]{:S(2)}) copy-start(bf16[4096,128]{1,0:T(8,128)(2,1)} %param.14) | copy-start | bytes 3145732
Sparse Core Ops, SparseCore 0:
  131.5 67.0 all-gather.1
  348.8 185.6 reduce-scatter.1
